TPU v7x, 32 devices: a whole 2x2x4 slice. The times are simulated.
32 devices in a mesh: groups: 1, tok: 32 (over z, y, x, core).
Axes of the slice: x: 2, y: 2, z: 4, core: 2. Of those that a mesh axis runs over, the one named last changes fastest.
Arguments:
- acts: bfloat16 [8192, 8192], P(('groups', 'tok')), may hold values from -6 to 6
- grads_out: bfloat16 [8192, 8192], P(('groups', 'tok')), may hold values from -6 to 6
- proj_in: bfloat16 [8192, 64], replicated, may hold values from -0.0625 to 0.0625
- proj_out: bfloat16 [8192, 64], replicated, may hold values from -0.0625 to 0.0625
- lengths: int32 [32], P('groups'), may hold values from 64 to 1024, as said below
- owned: int32 [32], P(('groups', 'tok')), may hold values from 0 to 31, each once
- queries: bfloat16 [128, 4096], P(('groups', 'tok')), may hold values from -6 to 6
Outputs:
- scores: float32 [32, 128], P(('groups', 'tok'))
Inputs may be any that keep to these rules, and one draw needn't show every extreme that they name: Sequence 0 has 1024 tokens, sequence 1 has 255, sequences 2 to 5 have 64 each, and all lengths sum to 8192; so no shard of 256 tokens touches more than 5 sequences, and the sixth shard touches exactly 5. `owned`: every sequence index appears exactly once.
All inputs are finite; a program needn't handle non-finite values.
Results may differ from a plain program's by a relative error of at most 0.0029.
Values may be sent and summed in bfloat16 or wider, within the bound.
A program may use at most 64 MiB of HBM per device.

v0:
```python
import jax
import jax.numpy as jnp
from jax import lax
from jax.sharding import PartitionSpec as P

PIECES = 5


def against_queries(matrix, queries):
    return jnp.dot(
        matrix,
        lax.all_gather(queries, "tok", axis=0, tiled=True).astype(jnp.float32).T,
        precision=lax.Precision.HIGHEST,
    )


def on_device(acts, grads_out, proj_in, proj_out, lengths, owned, queries):
    tok_rows = acts.shape[0]
    proj_rank = proj_in.shape[1]
    seq_count = lengths.shape[0]
    seq_ends = jnp.cumsum(lengths)
    positions = lax.axis_index("tok") * tok_rows + jnp.arange(tok_rows, dtype=jnp.int32)
    seq_of = jnp.sum((seq_ends[None, :] <= positions[:, None]).astype(jnp.int32), axis=1)
    piece_ids = seq_of[0] + jnp.arange(PIECES, dtype=jnp.int32)
    member = (seq_of[:, None] == piece_ids[None, :]).astype(jnp.float32)
    act_proj = jnp.dot(acts, proj_in, preferred_element_type=jnp.float32)
    grad_proj = jnp.dot(grads_out, proj_out, preferred_element_type=jnp.float32)
    outer_terms = (grad_proj[:, :, None] * act_proj[:, None, :]).reshape(
        tok_rows, proj_rank * proj_rank
    )
    pieces = jnp.dot(member.T, outer_terms, precision=lax.Precision.HIGHEST).astype(jnp.bfloat16)
    seq_index = jnp.arange(seq_count, dtype=jnp.int32)
    length_vals = lengths.astype(jnp.float32)
    grad_piece = lax.all_gather(pieces, "tok", axis=0, tiled=True)
    id_piece = lax.all_gather(piece_ids, "tok", axis=0, tiled=True)
    hits_mask = (owned[:, None] == id_piece[None, :]).astype(jnp.float32)
    owned_grads = jnp.dot(
        hits_mask, grad_piece.astype(jnp.float32), precision=lax.Precision.HIGHEST
    )
    matches = owned[:, None] == seq_index[None, :]
    found_len = jnp.sum(jnp.where(matches, length_vals[None, :], 0.0), axis=1)
    owned_grads = owned_grads * (1.0 / (proj_rank * jnp.sqrt(jnp.maximum(found_len, 1.0))))[:, None]
    return against_queries(owned_grads, queries)


def solution(mesh):
    return jax.shard_map(
        on_device,
        mesh=mesh,
        in_specs=(
            P(("groups", "tok"), None),
            P(("groups", "tok"), None),
            P(),
            P(),
            P("groups"),
            P(("groups", "tok")),
            P(("groups", "tok"), None),
        ),
        out_specs=P(("groups", "tok"), None),
        check_vma=False,
    )
```

profile of v0, /device:TPU:0, one launch (start us, length us, event | category | flops | bytes accessed | tf_op | source)
XLA Modules:
  0.0 135.5 jit_solution(224962681998372888)
XLA Ops:
  6.5 0.0 copy-start
  6.5 0.0 copy-start.2
  6.5 0.0 all-gather.7.cloned.1.call-start
  6.5 0.7 all-gather.7.cloned.1.call-update
  7.3 0.0 all-gather.5.cloned.1.call-start
  7.3 0.7 copy.13
  8.1 0.1 reduce-window.8
  8.1 0.1 reduce.2
  8.2 0.0 copy-start.1
  8.2 0.1 convert_reduce_fusion
  8.3 0.5 slice.3
  8.8 1.0 iota_add_fusion.1
  9.8 0.0 copy-done
  9.8 3.6 %fusion.5 = f32[256,64]{0,1:T(8,128)S(1)} fusion(bf16[256,8192]{1,0:T(8,128)(2,1)} %param.8, bf16[8192,64]{0,1:T(8,128)(2,1)S(1)} %copy-done), kind=kOutput, calls=%fused_computation.14 | convolution fusion | flops 268435456 | bytes 5308416 | tf_op jit(solution)/shard_map/dot_general | solution.py:27
  13.4 0.0 copy-done.2
  13.4 0.0 copy-done.1
  13.4 1.4 %fusion.6 = f32[256,64]{0,1:T(8,128)S(1)} fusion(bf16[256,8192]{1,0:T(8,128)(2,1)S(1)} %copy-done.1, bf16[8192,64]{0,1:T(8,128)(2,1)S(1)} %copy-done.2), kind=kOutput, calls=%fused_computation.15 | convolution fusion | flops 268435456 | bytes 5308416 | tf_op jit(solution)/shard_map/dot_general | solution.py:26
  14.8 0.0 copy-start.3
  14.8 0.5 broadcast_multiply_fusion
  15.4 2.7 %fusion = bf16[1,5,4096]{2,1,0:T(8,128)(2,1)} fusion(f32[256,4096]{0,1:T(8,128)S(1)} %bitcast.21, s32[5]{0:T(128)S(1)} %iota_add_fusion.1, s32[256]{0:T(256)S(1)} %convert_reduce_fusion), kind=kOutput, calls=%fused_computation.1 | convolution fusion | flops 62937600 | bytes 4236308 | tf_op jit(solution)/shard_map/dot_general | solution.py:31
  18.0 0.0 all-gather.5.cloned.1.call-update
  18.7 0.7 fusion.4
  19.5 42.0 %all-reduce = s32[160]{0:T(256)S(1)} all-reduce(s32[160]{0:T(256)S(1)} %fusion.4), channel_id=1, replica_groups=mesh['groups'=1,'tok'=32] {'tok'}, use_global_device_ids=true, to_apply=%add | all-reduce | flops 160 | bytes 1280
  61.5 0.0 copy-done.3
  61.5 0.6 fusion.3
  62.8 4.0 %all-gather.7.cloned.1.call-done = bf16[32,4,4096]{2,1,0:T(4,128)(2,1)} async-done(((bf16[1,4,4096]{2,1,0:T(4,128)(2,1)}), bf16[32,4,4096]{2,1,0:T(4,128)(2,1)}) %all-gather.7.cloned.1.call-update) | async-done | bytes 1048592 | tf_op jit(solution)/shard_map/all_gather | solution.py:12
  66.8 1.3 reshape.73
  68.1 56.9 %all-gather.5.cloned.1.call-done = bf16[32,5,4096]{2,1,0:T(8,128)(2,1)} async-done(((bf16[1,5,4096]{2,1,0:T(8,128)(2,1)}), bf16[32,5,4096]{2,1,0:T(8,128)(2,1)}) %all-gather.5.cloned.1.call-update) | async-done | bytes 1310736 | tf_op jit(solution)/shard_map/all_gather | solution.py:34
  125.1 1.8 %reshape.71 = bf16[160,4096]{1,0:T(8,128)(2,1)S(1)} reshape(bf16[32,5,4096]{2,1,0:T(8,128)(2,1)} %all-gather.5.cloned.1.call-done) | data formatting | bytes 2621440
  126.9 0.3 fusion.7
  127.2 1.4 %fusion.8 = f32[1,128]{1,0:T(1,128)} fusion(f32[4096,1]{0,1:T(1,128)S(1)} %bitcast.23, bf16[128,4096]{1,0:T(8,128)(2,1)S(1)} %reshape.73), kind=kOutput, calls=%fused_computation.17 | convolution fusion | flops 6291456 | bytes 1065472 | tf_op jit(solution)/shard_map/dot_general | solution.py:10
  (5 shorter events, 0.0 us)
Async XLA Ops:
  6.5 3.3 %copy-start = (bf16[8192,64]{0,1:T(8,128)(2,1)S(1)}, bf16[8192,64]{0,1:T(8,128)(2,1)}, u32[]{:S(2)}) copy-start(bf16[8192,64]{0,1:T(8,128)(2,1)} %param.10) | copy-start | bytes 3145732
  6.5 6.9 %copy-start.2 = (bf16[8192,64]{0,1:T(8,128)(2,1)S(1)}, bf16[8192,64]{0,1:T(8,128)(2,1)}, u32[]{:S(2)}) copy-start(bf16[8192,64]{0,1:T(8,128)(2,1)} %param.9) | copy-start | bytes 3145732
  6.5 60.2 %all-gather.7.cloned.1.call-start = ((), (), s32[]{:S(2)}) async-start(), calls=%async_computation.1 | async-start | bytes 1081344 | tf_op jit(solution)/shard_map/all_gather | solution.py:12
  7.3 117.8 %all-gather.5.cloned.1.call-start = ((), (), s32[]{:S(2)}) async-start(), calls=%async_computation | async-start | bytes 2162688 | tf_op jit(solution)/shard_map/all_gather | solution.py:34
  8.2 5.2 %copy-start.1 = (bf16[256,8192]{1,0:T(8,128)(2,1)S(1)}, bf16[256,8192]{1,0:T(8,128)(2,1)}, u32[]{:S(2)}) copy-start(bf16[256,8192]{1,0:T(8,128)(2,1)} %param.7) | copy-start | bytes 12582916
  14.8 46.6 %copy-start.3 = (s32[32]{0:T(128)S(1)}, s32[32]{0:T(128)}, u32[]{:S(2)}) copy-start(s32[32]{0:T(128)} %param.11) | copy-start | bytes 388
Sparse Core Ops, SparseCore 0:
  10.2 56.5 all-gather.6
  69.6 55.3 all-gather.4
where the time goes:
time: 136 us; the launch traced here: 135 us
  waiting for transfers between devices  61.6 us (45%)
  blocking collectives  42 us (31%)
  between operations  14.9 us (11%)
  matrix products  9.38 us (7%)
  local copies, waits for them, and re-layouts  4.45 us (3%)
  other arithmetic  3.09 us (2%)
    all_gather x1, waiting for transfers between devices, on_device(): grad_piece = lax.all_gather(pieces, 'tok', axis=0, tiled=True)  56.9 us
    unnamed x1, blocking collectives  42 us
    all_gather x1, waiting for transfers between devices, against_queries(): lax.all_gather(queries, 'tok', axis=0, tiled=True).astype(jnp.float32)  3.98 us
    dot_general x1, matrix products, on_device(): grad_proj = jnp.dot(grads_out, proj_out, preferred_element_type=jnp.float32)  3.58 us
    unnamed x11, local copies, waits for them, and re-layouts  3.19 us
  transfers between devices with their start and end apart: 2, of which 2 were waited for; matrix products, arithmetic and copies ran while one was open for 10% of the time, Pallas kernels for 0%

commit v1 on v0

v1 whole, which is shorter than its diff:
```python
import functools

import jax
import jax.numpy as jnp
from jax import lax
from jax.experimental import pallas as pl
from jax.experimental.pallas import tpu as pltpu
from jax.sharding import PartitionSpec as P

GROUP = 8
ROWS = 8
CHUNKS = 8
NT = (((1,), (1,)), ((), ()))


def split_bf16(x, parts):
    out = []
    for _ in range(parts):
        head = x.astype(jnp.bfloat16)
        out.append(head)
        x = x - head.astype(jnp.float32)
    return out


def kernel(
    n, acts, grads, pin, pout, lengths, owned, queries, out,
    a_buf, g_buf, pi_buf, po_buf, q_f32, q_send, q_recv, q_mat_f32, q_mat,
    o_send, o_recv, o_mat, p_send, p_recv, s_send, s_recv,
    load_sem, q_ssem, q_rsem, o_ssem, o_rsem, p_ssem, p_rsem, s_ssem, s_rsem,
):
    me = lax.axis_index("tok")
    tok, width = a_buf.shape
    rank = pi_buf.shape[0]
    step = width // CHUNKS
    nq_dev = queries.shape[0]
    nq = nq_dev * n
    seqs = lengths.shape[1]
    flat = rank * rank
    span = flat // GROUP
    blocks = span // 128
    base = lax.div(me, GROUP) * GROUP
    slot = lax.rem(me, GROUP)

    loads = []
    for i in range(CHUNKS):
        cols = pl.ds(i * step, step)
        group = [
            pltpu.make_async_copy(src.at[:, cols], dst.at[:, cols], load_sem.at[i, j])
            for j, (src, dst) in enumerate(
                ((pout, po_buf), (grads, g_buf), (pin, pi_buf), (acts, a_buf))
            )
        ]
        for c in group:
            c.start()
        loads.append(group)

    barrier = pltpu.get_barrier_semaphore()

    def greet(i, _):
        pl.semaphore_signal(
            barrier, inc=1, device_id={"tok": lax.rem(me + i, n)},
            device_id_type=pl.DeviceIdType.MESH,
        )
        return 0

    lax.fori_loop(1, n, greet, 0)

    for a in range(GROUP):
        for b in range(blocks):
            q_f32[a, b * nq_dev:(b + 1) * nq_dev, :] = queries[
                :, (a * blocks + b) * 128:(a * blocks + b + 1) * 128
            ].astype(jnp.float32)
    q_send[...] = q_f32[...].astype(jnp.bfloat16)
    own = owned[0]
    o_send[...] = jnp.full(o_send.shape, own, jnp.int32)

    pl.semaphore_wait(barrier, n - 1)

    def send_queries(i, _):
        to = lax.rem(me + i, n)
        pltpu.make_async_remote_copy(
            q_send.at[lax.rem(to, GROUP)], q_recv.at[me], q_ssem, q_rsem,
            device_id={"tok": to}, device_id_type=pl.DeviceIdType.MESH,
        ).start()
        pltpu.make_async_remote_copy(
            o_send.at[0], o_recv.at[me], o_ssem, o_rsem,
            device_id={"tok": to}, device_id_type=pl.DeviceIdType.MESH,
        ).start()
        return 0

    lax.fori_loop(1, n, send_queries, 0)

    len_row = lengths[...].astype(jnp.float32)
    row_i = lax.broadcasted_iota(jnp.int32, (seqs, seqs), 0)
    col_i = lax.broadcasted_iota(jnp.int32, (seqs, seqs), 1)
    ends = jnp.sum(jnp.where(col_i <= row_i, len_row, 0.0), axis=1, keepdims=True)
    pos = (me * tok + lax.broadcasted_iota(jnp.int32, (1, tok), 1)).astype(jnp.float32)
    seq_of = jnp.sum((ends <= pos).astype(jnp.float32), axis=0, keepdims=True)
    start = (me * tok).astype(jnp.float32)
    first = jnp.sum((ends <= start).astype(jnp.float32), axis=0, keepdims=True)
    piece = lax.broadcasted_iota(jnp.int32, (ROWS, tok), 0).astype(jnp.float32)
    member = ((seq_of - first) == piece).astype(jnp.float32)
    lane = lax.broadcasted_iota(jnp.int32, (1, GROUP * ROWS), 1)
    shard_start = ((base + lane // ROWS) * tok).astype(jnp.float32)
    ids = jnp.sum((ends <= shard_start).astype(jnp.float32), axis=0, keepdims=True)
    ids = ids + (lane % ROWS).astype(jnp.float32)

    g_t = jnp.zeros((rank, tok), jnp.float32)
    a_t = jnp.zeros((rank, tok), jnp.float32)
    for i in range(CHUNKS):
        cols = pl.ds(i * step, step)
        loads[i][0].wait()
        loads[i][1].wait()
        g_t += lax.dot_general(
            po_buf[:, cols], g_buf[:, cols], NT, preferred_element_type=jnp.float32
        )
        loads[i][2].wait()
        loads[i][3].wait()
        a_t += lax.dot_general(
            pi_buf[:, cols], a_buf[:, cols], NT, preferred_element_type=jnp.float32
        )

    g_hi, g_lo = [
        (part.astype(jnp.float32)[:, None, :] * member[None]).reshape(rank * ROWS, tok)
        .astype(jnp.bfloat16)
        for part in split_bf16(g_t, 2)
    ]
    a_hi, a_lo = split_bf16(a_t, 2)
    both = jnp.concatenate([a_hi, a_hi, a_lo, a_lo], axis=0)
    m = lax.dot_general(g_hi, both, NT, preferred_element_type=jnp.float32)
    m = m[:, :2 * rank] + m[:, 2 * rank:] + lax.dot_general(
        g_lo, both[:2 * rank], NT, preferred_element_type=jnp.float32
    )
    m = m.reshape(rank // 2, 2, ROWS, 2 * rank)
    low = lax.broadcasted_iota(jnp.int32, (1, 1, 2 * rank), 2) < rank
    flat_piece = jnp.where(low, m[:, 0], m[:, 1])
    half = blocks // 2
    flat_piece = flat_piece.reshape(GROUP, 2, half, ROWS, 128)
    for b in range(half):
        p_send[:, :, b * 128:(b + 1) * 128] = (
            flat_piece[:, :, b].reshape(GROUP, 2 * ROWS, 128).astype(jnp.bfloat16)
        )

    def send_pieces(i, _):
        to = lax.rem(slot + i, GROUP)
        pltpu.make_async_remote_copy(
            p_send.at[to], p_recv.at[slot], p_ssem, p_rsem,
            device_id={"tok": base + to}, device_id_type=pl.DeviceIdType.MESH,
        ).start()
        return 0

    lax.fori_loop(1, GROUP, send_pieces, 0)
    p_recv[slot] = p_send[slot]

    others = pl.ds(0, n - 1)
    pltpu.make_async_copy(q_recv.at[others], q_recv.at[others], q_rsem).wait()
    pltpu.make_async_copy(o_recv.at[others], o_recv.at[others], o_rsem).wait()
    q_recv[me] = q_send[slot]
    o_recv[me] = o_send[0]
    for k in range(n):
        block = q_recv[k].astype(jnp.float32)
        for b in range(blocks):
            h, i = divmod(b, half)
            q_mat_f32[h * nq + k * nq_dev:h * nq + (k + 1) * nq_dev, i * 128:(i + 1) * 128] = (
                block[b * nq_dev:(b + 1) * nq_dev]
            )
        o_mat[k:k + 1, :] = o_recv[k].astype(jnp.float32)
    q_mat[...] = q_mat_f32[...].astype(jnp.bfloat16)
    wants = (o_mat[:, :GROUP * ROWS] == ids).astype(jnp.bfloat16)

    peers = pl.ds(0, GROUP - 1)
    pltpu.make_async_copy(p_recv.at[peers], p_recv.at[peers], p_rsem).wait()
    x = p_recv[...].reshape(GROUP * 2 * ROWS, half * 128)
    y = lax.dot_general(x, q_mat[...], NT, preferred_element_type=jnp.float32)
    y = y.reshape(GROUP, 2, ROWS, 2 * nq)
    part = (y[:, 0, :, :nq] + y[:, 1, :, nq:]).reshape(GROUP * ROWS, nq)
    rows = jnp.dot(
        jnp.concatenate([wants] * 3, axis=1),
        jnp.concatenate(split_bf16(part, 3), axis=0),
        preferred_element_type=jnp.float32,
    )
    for k in range(n):
        s_send[k] = rows[k:k + 1, :]

    def send_scores(i, _):
        to = lax.rem(me + i, n)
        pltpu.make_async_remote_copy(
            s_send.at[to], s_recv.at[me], s_ssem, s_rsem,
            device_id={"tok": to}, device_id_type=pl.DeviceIdType.MESH,
        ).start()
        return 0

    lax.fori_loop(1, n, send_scores, 0)
    s_recv[me] = s_send[me]

    seq = lax.broadcasted_iota(jnp.int32, (1, seqs), 1)
    found = jnp.sum(jnp.where(seq == own, len_row, 0.0), axis=1, keepdims=True)
    scale = 1.0 / (rank * jnp.sqrt(jnp.maximum(found, 1.0)))

    pltpu.make_async_copy(s_recv.at[others], s_recv.at[others], s_rsem).wait()
    out[...] = jnp.sum(s_recv[...], axis=0) * scale

    pltpu.make_async_copy(q_recv.at[others], q_recv.at[others], q_ssem).wait()
    pltpu.make_async_copy(o_recv.at[others], o_recv.at[others], o_ssem).wait()
    pltpu.make_async_copy(p_recv.at[peers], p_recv.at[peers], p_ssem).wait()
    pltpu.make_async_copy(s_recv.at[others], s_recv.at[others], s_ssem).wait()


def on_device(n, acts, grads_out, proj_in, proj_out, lengths, owned, queries):
    tok, width = acts.shape
    rank = proj_in.shape[1]
    nq_dev = queries.shape[0]
    nq = nq_dev * n
    span = rank * rank // GROUP
    q_rows = nq_dev * span // 128
    bf16, f32, i32 = jnp.bfloat16, jnp.float32, jnp.int32
    hbm = pl.BlockSpec(memory_space=pl.ANY)
    vmem = pl.BlockSpec(memory_space=pltpu.VMEM)
    smem = pl.BlockSpec(memory_space=pltpu.SMEM)
    return pl.pallas_call(
        functools.partial(kernel, n),
        out_shape=jax.ShapeDtypeStruct((1, nq), f32),
        in_specs=[hbm, hbm, hbm, hbm, vmem, smem, vmem],
        out_specs=vmem,
        scratch_shapes=[
            pltpu.VMEM((tok, width), bf16),
            pltpu.VMEM((tok, width), bf16),
            pltpu.VMEM((rank, width), bf16),
            pltpu.VMEM((rank, width), bf16),
            pltpu.VMEM((GROUP, q_rows, 128), f32),
            pltpu.VMEM((GROUP, q_rows, 128), bf16),
            pltpu.VMEM((n, q_rows, 128), bf16),
            pltpu.VMEM((2 * nq, span // 2), f32),
            pltpu.VMEM((2 * nq, span // 2), bf16),
            pltpu.VMEM((1, 1, 128), i32),
            pltpu.VMEM((n, 1, 128), i32),
            pltpu.VMEM((n, 128), f32),
            pltpu.VMEM((GROUP, 2 * ROWS, span // 2), bf16),
            pltpu.VMEM((GROUP, 2 * ROWS, span // 2), bf16),
            pltpu.VMEM((n, 1, nq), f32),
            pltpu.VMEM((n, 1, nq), f32),
            pltpu.SemaphoreType.DMA((CHUNKS, 4)),
        ] + [pltpu.SemaphoreType.DMA] * 8,
        compiler_params=pltpu.CompilerParams(
            collective_id=0, has_side_effects=True, vmem_limit_bytes=48 * 1024 * 1024
        ),
    )(acts, grads_out, proj_in.T, proj_out.T, lengths.reshape(1, -1), owned, queries)


def solution(mesh):
    return jax.shard_map(
        functools.partial(on_device, mesh.shape["tok"]),
        mesh=mesh,
        in_specs=(
            P(("groups", "tok"), None),
            P(("groups", "tok"), None),
            P(),
            P(),
            P("groups"),
            P(("groups", "tok")),
            P(("groups", "tok"), None),
        ),
        out_specs=P(("groups", "tok"), None),
        check_vma=False,
    )
```

time: 136 us -> 25.6 us (0.19)
  waiting for transfers between devices: 61.6 us -> 0 us
  blocking collectives: 42 us -> 0 us
  Pallas kernels: 0 us -> 20.3 us
  between operations: 14.9 us -> 0.67 us
  matrix products: 9.38 us -> 0 us
  other arithmetic: 3.09 us -> 0 us
    all_gather x2 -> x0, waiting for transfers between devices: 60.9 us -> none  [the longest x1 56.9 us: on_device(): grad_piece = lax.all_gather(pieces, 'tok', axis=0, tiled=True)]
    unnamed x1 -> x0, blocking collectives: 42 us -> none
    pallas_call x0 -> x1, Pallas kernels: none -> 20.3 us  [on_device(): pl.pallas_call(functools.partial(kernel, n), out_shape=jax.ShapeDtypeStru...]
    dot_general x5 -> x0, matrix products: 9.38 us -> none  [the longest x1 3.58 us: on_device(): grad_proj = jnp.dot(grads_out, proj_out, preferred_element_type=jnp.float32)]
    unnamed x11 -> x9, local copies, waits for them, and re-layouts: 3.19 us -> 4.37 us
  transfers between devices with their start and end apart: 2 -> 0, of which waited for: 2 -> 0; matrix products, arithmetic and copies ran while one was open for 10% -> 0% of each run, Pallas kernels for 0% -> 0%
where the time goes in v1:
time: 25.6 us; the launch traced here: 25.4 us
  Pallas kernels  20.3 us (79%)
  local copies, waits for them, and re-layouts  4.37 us (17%)
  between operations  0.67 us (3%)
    pallas_call x1, Pallas kernels, on_device(): pl.pallas_call(functools.partial(kernel, n), out_shape=jax.ShapeDtypeStru...  20.3 us
    unnamed x9, local copies, waits for them, and re-layouts  4.37 us

profile of v1, /device:TPU:0, one launch (start us, length us, event | category | flops | bytes accessed | tf_op | source)
XLA Modules:
  0.0 25.4 jit_solution(7701737256655263704)
XLA Ops:
  0.7 0.0 copy-start
  0.7 1.2 %copy-done = bf16[8192,64]{0,1:T(8,128)(2,1)S(1)} copy-done((bf16[8192,64]{0,1:T(8,128)(2,1)S(1)}, bf16[8192,64]{0,1:T(8,128)(2,1)}, u32[]{:S(2)}) %copy-start) | copy-done | bytes 1048600
  1.9 0.0 copy-start.1
  1.9 1.2 %copy-done.1 = bf16[8192,64]{0,1:T(8,128)(2,1)S(1)} copy-done((bf16[8192,64]{0,1:T(8,128)(2,1)S(1)}, bf16[8192,64]{0,1:T(8,128)(2,1)}, u32[]{:S(2)}) %copy-start.1) | copy-done | bytes 1048600
  3.1 0.0 copy-start.2
  3.1 0.8 %copy-done.2 = bf16[4,4096]{1,0:T(4,128)(2,1)S(1)} copy-done((bf16[4,4096]{1,0:T(4,128)(2,1)S(1)}, bf16[4,4096]{1,0:T(4,128)(2,1)}, u32[]{:S(2)}) %copy-start.2) | copy-done | bytes 32792
  3.9 0.0 copy-start.3
  3.9 0.7 %copy-done.3 = s32[32]{0:T(128)S(1)} copy-done((s32[32]{0:T(128)S(1)}, s32[32]{0:T(128)}, u32[]{:S(2)}) %copy-start.3) | copy-done | bytes 152
  4.5 20.3 %shard_map.73 = f32[1,128]{1,0:T(1,128)S(1)} custom-call(bf16[256,8192]{1,0:T(8,128)(2,1)} %acts.1, bf16[256,8192]{1,0:T(8,128)(2,1)} %grads.1, bf16[64,8192]{1,0:T(8,128)(2,1)S(1)} %bitcast.3, bf16[64,8192]{1,0:T(8,128)(2,1)S(1)} %bitcast.4, s32[1,32]{1,0:T(1,128)S(1)} %bitcast.5, s32[1]{0:T(128)S(6)} %copy.9.owned, bf16[4,4096]{1,0:T(4,128)(2,1)S(1)} %copy-done.2), custom_call_target="tpu_custom_call" | custom-call | tf_op jit(solution)/shard_map/pallas_call | solution.py:220
  24.8 0.5 %copy.10 = f32[1,128]{1,0:T(1,128)} copy(f32[1,128]{1,0:T(1,128)S(1)} %shard_map.73) | data formatting | bytes 1024
Async XLA Ops:
  0.7 1.2 %copy-start = (bf16[8192,64]{0,1:T(8,128)(2,1)S(1)}, bf16[8192,64]{0,1:T(8,128)(2,1)}, u32[]{:S(2)}) copy-start(bf16[8192,64]{0,1:T(8,128)(2,1)} %param.9) | copy-start | bytes 3145732
  1.9 1.2 %copy-start.1 = (bf16[8192,64]{0,1:T(8,128)(2,1)S(1)}, bf16[8192,64]{0,1:T(8,128)(2,1)}, u32[]{:S(2)}) copy-start(bf16[8192,64]{0,1:T(8,128)(2,1)} %param.10) | copy-start | bytes 3145732
  3.1 0.8 %copy-start.2 = (bf16[4,4096]{1,0:T(4,128)(2,1)S(1)}, bf16[4,4096]{1,0:T(4,128)(2,1)}, u32[]{:S(2)}) copy-start(bf16[4,4096]{1,0:T(4,128)(2,1)} %queries.1) | copy-start | bytes 98308
  3.9 0.7 %copy-start.3 = (s32[32]{0:T(128)S(1)}, s32[32]{0:T(128)}, u32[]{:S(2)}) copy-start(s32[32]{0:T(128)} %param.11) | copy-start | bytes 388

commit v2 on v1

--- a/solution.py
+++ b/solution.py
@@ -9,7 +9,9 @@
 
 GROUP = 8
 ROWS = 8
-CHUNKS = 8
+CHUNKS = 1
+MEET = 0
+VMEM_LIMIT = 62 * 1024 * 1024
 NT = (((1,), (1,)), ((), ()))
 
 
@@ -23,10 +25,10 @@
 
 
 def kernel(
-    n, acts, grads, pin, pout, lengths, owned, queries, out,
-    a_buf, g_buf, pi_buf, po_buf, q_f32, q_send, q_recv, q_mat_f32, q_mat,
+    n, acts, grads, pin, pout, lengths_hbm, owned, queries_hbm, out,
+    lengths, queries, a_buf, g_buf, pi_buf, po_buf, q_f32, q_send, q_recv, q_mat_f32, q_mat,
     o_send, o_recv, o_mat, p_send, p_recv, s_send, s_recv,
-    load_sem, q_ssem, q_rsem, o_ssem, o_rsem, p_ssem, p_rsem, s_ssem, s_rsem,
+    small_sem, load_sem, q_ssem, q_rsem, o_ssem, o_rsem, p_ssem, p_rsem, s_ssem, s_rsem,
 ):
     me = lax.axis_index("tok")
     tok, width = a_buf.shape
@@ -41,6 +43,12 @@
     base = lax.div(me, GROUP) * GROUP
     slot = lax.rem(me, GROUP)
 
+    small = [
+        pltpu.make_async_copy(queries_hbm, queries, small_sem.at[0]),
+        pltpu.make_async_copy(lengths_hbm, lengths, small_sem.at[1]),
+    ]
+    for c in small:
+        c.start()
     loads = []
     for i in range(CHUNKS):
         cols = pl.ds(i * step, step)
@@ -63,8 +71,10 @@
         )
         return 0
 
-    lax.fori_loop(1, n, greet, 0)
-
+    lax.fori_loop(1, n, greet, 0, unroll=True)
+
+    small[0].wait()
+    small[1].wait()
     for a in range(GROUP):
         for b in range(blocks):
             q_f32[a, b * nq_dev:(b + 1) * nq_dev, :] = queries[
@@ -74,8 +84,6 @@
     own = owned[0]
     o_send[...] = jnp.full(o_send.shape, own, jnp.int32)
 
-    pl.semaphore_wait(barrier, n - 1)
-
     def send_queries(i, _):
         to = lax.rem(me + i, n)
         pltpu.make_async_remote_copy(
@@ -87,8 +95,6 @@
             device_id={"tok": to}, device_id_type=pl.DeviceIdType.MESH,
         ).start()
         return 0
-
-    lax.fori_loop(1, n, send_queries, 0)
 
     len_row = lengths[...].astype(jnp.float32)
     row_i = lax.broadcasted_iota(jnp.int32, (seqs, seqs), 0)
@@ -108,6 +114,9 @@
     g_t = jnp.zeros((rank, tok), jnp.float32)
     a_t = jnp.zeros((rank, tok), jnp.float32)
     for i in range(CHUNKS):
+        if i == MEET:
+            pl.semaphore_wait(barrier, n - 1)
+            lax.fori_loop(1, n, send_queries, 0, unroll=True)
         cols = pl.ds(i * step, step)
         loads[i][0].wait()
         loads[i][1].wait()
@@ -149,7 +158,7 @@
         ).start()
         return 0
 
-    lax.fori_loop(1, GROUP, send_pieces, 0)
+    lax.fori_loop(1, GROUP, send_pieces, 0, unroll=True)
     p_recv[slot] = p_send[slot]
 
     others = pl.ds(0, n - 1)
@@ -190,7 +199,7 @@
         ).start()
         return 0
 
-    lax.fori_loop(1, n, send_scores, 0)
+    lax.fori_loop(1, n, send_scores, 0, unroll=True)
     s_recv[me] = s_send[me]
 
     seq = lax.broadcasted_iota(jnp.int32, (1, seqs), 1)
@@ -207,6 +216,7 @@
 
 
 def on_device(n, acts, grads_out, proj_in, proj_out, lengths, owned, queries):
+    lengths = lengths.reshape(1, -1)
     tok, width = acts.shape
     rank = proj_in.shape[1]
     nq_dev = queries.shape[0]
@@ -214,15 +224,17 @@
     span = rank * rank // GROUP
     q_rows = nq_dev * span // 128
     bf16, f32, i32 = jnp.bfloat16, jnp.float32, jnp.int32
-    hbm = pl.BlockSpec(memory_space=pl.ANY)
+    hbm = pl.BlockSpec(memory_space=pltpu.HBM)
     vmem = pl.BlockSpec(memory_space=pltpu.VMEM)
     smem = pl.BlockSpec(memory_space=pltpu.SMEM)
     return pl.pallas_call(
         functools.partial(kernel, n),
         out_shape=jax.ShapeDtypeStruct((1, nq), f32),
-        in_specs=[hbm, hbm, hbm, hbm, vmem, smem, vmem],
+        in_specs=[hbm, hbm, hbm, hbm, hbm, smem, hbm],
         out_specs=vmem,
         scratch_shapes=[
+            pltpu.VMEM(lengths.shape, i32),
+            pltpu.VMEM(queries.shape, bf16),
             pltpu.VMEM((tok, width), bf16),
             pltpu.VMEM((tok, width), bf16),
             pltpu.VMEM((rank, width), bf16),
@@ -239,12 +251,13 @@
             pltpu.VMEM((GROUP, 2 * ROWS, span // 2), bf16),
             pltpu.VMEM((n, 1, nq), f32),
             pltpu.VMEM((n, 1, nq), f32),
+            pltpu.SemaphoreType.DMA((2,)),
             pltpu.SemaphoreType.DMA((CHUNKS, 4)),
         ] + [pltpu.SemaphoreType.DMA] * 8,
         compiler_params=pltpu.CompilerParams(
-            collective_id=0, has_side_effects=True, vmem_limit_bytes=48 * 1024 * 1024
+            collective_id=0, has_side_effects=True, vmem_limit_bytes=VMEM_LIMIT
         ),
-    )(acts, grads_out, proj_in.T, proj_out.T, lengths.reshape(1, -1), owned, queries)
+    )(acts, grads_out, proj_in.T, proj_out.T, lengths, owned, queries)
 
 
 def solution(mesh):

time: 25.6 us -> 21.7 us (0.85)
  local copies, waits for them, and re-layouts: 4.37 us -> 1.19 us
  Pallas kernels: 20.3 us -> 19.7 us
    unnamed x9 -> x1, local copies, waits for them, and re-layouts: 4.37 us -> 1.19 us
    pallas_call x1, Pallas kernels: 20.3 us -> 19.7 us  [on_device(): pl.pallas_call(functools.partial(kernel, n), out_shape=jax.ShapeDtypeStru...]
where the time goes in v2:
time: 21.7 us; the launch traced here: 21.5 us
  Pallas kernels  19.7 us (91%)
  local copies, waits for them, and re-layouts  1.19 us (5%)
  between operations  0.66 us (3%)
    pallas_call x1, Pallas kernels, on_device(): pl.pallas_call(functools.partial(kernel, n), out_shape=jax.ShapeDtypeStru...  19.7 us
    unnamed x1, local copies, waits for them, and re-layouts  1.19 us

profile of v2, /device:TPU:0, one launch (start us, length us, event | category | flops | bytes accessed | tf_op | source)
XLA Modules:
  0.0 21.5 jit_solution(16251853448674654874)
XLA Ops:
  0.7 19.7 %shard_map.73 = f32[1,128]{1,0:T(1,128)} custom-call(bf16[256,8192]{1,0:T(8,128)(2,1)} %acts.1, bf16[256,8192]{1,0:T(8,128)(2,1)} %grads.1, bf16[64,8192]{1,0:T(8,128)(2,1)} %bitcast.3, bf16[64,8192]{1,0:T(8,128)(2,1)} %bitcast.4, s32[1,32]{1,0:T(1,128)} %bitcast.5, s32[1]{0:T(128)S(6)} %copy.9.owned, bf16[4,4096]{1,0:T(4,128)(2,1)} %queries_hbm.1), custom_call_target="tpu_custom_call" | custom-call | tf_op jit(solution)/shard_map/pallas_call | solution.py:230
  20.3 1.2 %copy.10 = f32[1,128]{1,0:T(1,128)} copy(f32[1,128]{1,0:T(1,128)} %shard_map.73) | data formatting | bytes 1024

commit v3 on v2

--- a/solution.py
+++ b/solution.py
@@ -43,6 +43,17 @@
     base = lax.div(me, GROUP) * GROUP
     slot = lax.rem(me, GROUP)
 
+    barrier = pltpu.get_barrier_semaphore()
+
+    def greet(i, _):
+        pl.semaphore_signal(
+            barrier, inc=1, device_id={"tok": lax.rem(me + i, n)},
+            device_id_type=pl.DeviceIdType.MESH,
+        )
+        return 0
+
+    lax.fori_loop(1, n, greet, 0, unroll=True)
+
     small = [
         pltpu.make_async_copy(queries_hbm, queries, small_sem.at[0]),
         pltpu.make_async_copy(lengths_hbm, lengths, small_sem.at[1]),
@@ -61,17 +72,6 @@
         for c in group:
             c.start()
         loads.append(group)
-
-    barrier = pltpu.get_barrier_semaphore()
-
-    def greet(i, _):
-        pl.semaphore_signal(
-            barrier, inc=1, device_id={"tok": lax.rem(me + i, n)},
-            device_id_type=pl.DeviceIdType.MESH,
-        )
-        return 0
-
-    lax.fori_loop(1, n, greet, 0, unroll=True)
 
     small[0].wait()
     small[1].wait()

time: 21.7 us -> 21.9 us (level)
  no operation moved by 1% of the time
where the time goes in v3:
time: 21.9 us; the launch traced here: 21.8 us
  Pallas kernels  19.9 us (91%)
  local copies, waits for them, and re-layouts  1.19 us (5%)
  between operations  0.66 us (3%)
    pallas_call x1, Pallas kernels, on_device(): pl.pallas_call(functools.partial(kernel, n), out_shape=jax.ShapeDtypeStru...  19.9 us
    unnamed x1, local copies, waits for them, and re-layouts  1.19 us

profile of v3, /device:TPU:0, one launch (start us, length us, event | category | flops | bytes accessed | tf_op | source)
XLA Modules:
  0.0 21.8 jit_solution(14099252880107773479)
XLA Ops:
  0.7 19.9 %shard_map.73 = f32[1,128]{1,0:T(1,128)} custom-call(bf16[256,8192]{1,0:T(8,128)(2,1)} %acts.1, bf16[256,8192]{1,0:T(8,128)(2,1)} %grads.1, bf16[64,8192]{1,0:T(8,128)(2,1)} %bitcast.3, bf16[64,8192]{1,0:T(8,128)(2,1)} %bitcast.4, s32[1,32]{1,0:T(1,128)} %bitcast.5, s32[1]{0:T(128)S(6)} %copy.9.owned, bf16[4,4096]{1,0:T(4,128)(2,1)} %queries_hbm.1), custom_call_target="tpu_custom_call" | custom-call | tf_op jit(solution)/shard_map/pallas_call | solution.py:230
  20.6 1.2 %copy.10 = f32[1,128]{1,0:T(1,128)} copy(f32[1,128]{1,0:T(1,128)} %shard_map.73) | data formatting | bytes 1024
